TPU v7x, 1024 devices: a whole 4x8x16 slice. The times are simulated.
1024 devices in a mesh: dp: 128 (over z, y_lo, core), fsdp: 8 (over y_hi, x).
Axes of the slice: x: 4, y: 8 (y_hi: 2, y_lo: 4; y = y_hi * 4 + y_lo), z: 16, core: 2. Of those that a mesh axis runs over, the one named last changes fastest.
Arguments:
- acts: bfloat16 [49152, 8192], P('dp', 'fsdp'), may hold values from -6 to 6
- grad_out: bfloat16 [49152, 2048], P('dp'), may hold values from -0.109375 to 0.109375
- basis: bfloat16 [8192, 1024], P('fsdp'), may hold values from -0.0625 to 0.0625
- master: float32 [2048, 8192], P('dp', 'fsdp'), may hold values from -0.12 to 0.12
- exp_avg: float32 [2048, 1024], P('dp', 'fsdp'), may hold values from -1.8 to 1.8
- exp_avg_sq: float32 [2048, 1024], P('dp', 'fsdp'), may hold values from 0.05 to 2
Outputs:
- new_master: float32 [2048, 8192], P('dp', 'fsdp')
- new_weight: bfloat16 [2048, 8192], P(None, 'fsdp')
- new_avg: float32 [2048, 1024], P('dp', 'fsdp')
- new_avg_sq: float32 [2048, 1024], P('dp', 'fsdp')
All inputs are finite; a program needn't handle non-finite values.
Results may differ from a plain program's by a relative error of at most 0.0022.
Values may be sent and summed in bfloat16 or wider, within the bound.
A program may use at most 32 MiB of HBM per device.

v0:
```python
import jax
import jax.numpy as jnp
from jax import lax
from jax.sharding import PartitionSpec as P


def on_device(acts, grad_out, basis, master, exp_avg, exp_avg_sq):
    groups = lax.axis_size("fsdp")
    share = basis.shape[1] // groups
    partial_sum = lax.dot_general(
        basis, acts, (((0,), (1,)), ((), ())), preferred_element_type=jnp.float32
    )
    summed = lax.psum(partial_sum, "fsdp")
    mine = lax.dynamic_slice_in_dim(summed, lax.axis_index("fsdp") * share, share, 0)
    proj_rows = mine.astype(jnp.bfloat16)
    local_grad = lax.dot_general(
        grad_out, proj_rows, (((0,), (1,)), ((), ())), preferred_element_type=jnp.float32
    )
    proj_grad = lax.psum_scatter(local_grad, "dp", scatter_dimension=0, tiled=True)
    new_avg = 0.9 * exp_avg + 0.1 * proj_grad
    new_avg_sq = 0.95 * exp_avg_sq + 0.05 * proj_grad * proj_grad
    first_fix = 1.0 - 0.9**20
    second_fix = 1.0 - 0.95**20
    direction = (new_avg / first_fix / (jnp.sqrt(new_avg_sq / second_fix) + 1e-08)).astype(
        jnp.bfloat16
    )
    full_direction = lax.all_gather(direction, "fsdp", axis=1, tiled=True)
    delta = lax.dot_general(
        full_direction, basis, (((1,), (1,)), ((), ())), preferred_element_type=jnp.float32
    )
    new_master = master - 0.0125 * delta
    new_weight = lax.all_gather(new_master.astype(jnp.bfloat16), "dp", axis=0, tiled=True)
    return (new_master, new_weight, new_avg, new_avg_sq)


def solution(mesh):
    return jax.shard_map(
        on_device,
        mesh=mesh,
        in_specs=(
            P("dp", "fsdp"),
            P("dp", None),
            P("fsdp", None),
            P("dp", "fsdp"),
            P("dp", "fsdp"),
            P("dp", "fsdp"),
        ),
        out_specs=(P("dp", "fsdp"), P(None, "fsdp"), P("dp", "fsdp"), P("dp", "fsdp")),
        check_vma=False,
    )
```

profile of v0, /device:TPU:1, one launch (start us, length us, event | category | flops | bytes accessed | tf_op | source)
XLA Modules:
  0.0 963.7 jit_solution(3768398042912714283)
XLA Ops:
  7.2 0.0 copy-start
  7.2 0.0 reduce-scatter.4.cloned.1.call-start
  7.2 1.5 copy-done
  8.8 3.6 fusion.5
  12.3 109.1 %all-reduce.1 = bf16[1024,384]{1,0:T(8,128)(2,1)} all-reduce(f32[1024,384]{1,0:T(8,128)} %fusion.5), channel_id=1, replica_groups=mesh['dp'=128,'fsdp'=8] {'fsdp'}, use_global_device_ids=true, to_apply=%region_0.0 | all-reduce | flops 393216 | bytes 2359296 | tf_op jit(solution)/shard_map/psum | solution.py:13
  121.4 1.9 convolution_bitcast_fusion
  123.3 0.0 copy-start.2
  123.4 0.0 copy-start.3
  123.4 0.0 copy-start.1
  123.4 1.3 copy.25
  124.7 0.0 reduce-scatter.4.cloned.1.call-update
  124.7 0.0 all-gather.2.cloned.1.call-start
  124.8 560.6 %reduce-scatter.4.cloned.1.call-done = f32[16,128]{1,0:T(8,128)} async-done(((f32[2048,128]{1,0:T(8,128)}), f32[16,128]{1,0:T(8,128)}) %reduce-scatter.4.cloned.1.call-update) | async-done | bytes 8208 | tf_op jit(solution)/shard_map/reduce_scatter | solution.py:19
  685.3 0.0 copy-done.2
  685.3 0.0 copy-done.3
  685.3 1.3 divide_convert_fusion
  686.7 34.7 %all_gather.6 = bf16[16,1024]{1,0:T(8,128)(2,1)S(1)} all-gather(bf16[16,128]{1,0:T(8,128)(2,1)S(1)} %get-tuple-element.12), channel_id=1, replica_groups=mesh['dp'=128,'fsdp'=8] {'fsdp'}, dimensions={1}, use_global_device_ids=true | all-gather | bytes 36864 | tf_op jit(solution)/shard_map/all_gather | solution.py:27
  721.4 0.0 copy-done.1
  721.4 1.3 fusion.4
  722.7 0.0 all-gather.2.cloned.1.call-update
  722.7 229.5 %all-gather.2.cloned.1.call-done = bf16[2048,1024]{1,0:T(8,128)(2,1)} async-done(((bf16[16,1024]{1,0:T(8,128)(2,1)}), bf16[2048,1024]{1,0:T(8,128)(2,1)}) %all-gather.2.cloned.1.call-update) | async-done | bytes 4194320 | tf_op jit(solution)/shard_map/all_gather | solution.py:32
  952.2 4.6 copy.30
Async XLA Ops:
  7.2 1.6 copy-start
  7.2 678.2 %reduce-scatter.4.cloned.1.call-start = ((), (), s32[]{:S(2)}) async-start(), calls=%async_computation.2 | async-start | bytes 1056768 | tf_op jit(solution)/shard_map/reduce_scatter | solution.py:19
  123.3 562.0 %copy-start.2 = (f32[16,128]{1,0:T(8,128)S(1)}, f32[16,128]{1,0:T(8,128)}, u32[]{:S(2)}) copy-start(f32[16,128]{1,0:T(8,128)} %param.10) | copy-start | bytes 24580
  123.4 562.0 %copy-start.3 = (f32[16,128]{1,0:T(8,128)S(1)}, f32[16,128]{1,0:T(8,128)}, u32[]{:S(2)}) copy-start(f32[16,128]{1,0:T(8,128)} %param.11) | copy-start | bytes 24580
  123.4 598.0 %copy-start.1 = (f32[16,1024]{1,0:T(8,128)S(1)}, f32[16,1024]{1,0:T(8,128)}, u32[]{:S(2)}) copy-start(f32[16,1024]{1,0:T(8,128)} %param.9) | copy-start | bytes 196612
  124.7 827.5 %all-gather.2.cloned.1.call-start = ((), (), s32[]{:S(2)}) async-start(), calls=%async_computation.1 | async-start | bytes 4227072 | tf_op jit(solution)/shard_map/all_gather | solution.py:32
Sparse Core Ops, SparseCore 0:
  124.8 560.4 reduce-scatter.3
  722.8 229.3 all-gather.1
where the time goes:
time: 964 us
  waiting for transfers between devices  790 us (82%)
  blocking collectives  144 us (15%)
  between operations  14.1 us (1%)
    reduce_scatter x1, waiting for transfers between devices, on_device(): lax.psum_scatter(local_grad, 'dp', scatter_dimension=0, tiled=True)  561 us
    all_gather x1, waiting for transfers between devices, on_device(): lax.all_gather(new_master.astype(jnp.bfloat16), 'dp', axis=0, tiled=True)  230 us
    psum x1, blocking collectives, on_device(): summed = lax.psum(partial_sum, 'fsdp')  109 us
    all_gather x1, blocking collectives, on_device(): full_direction = lax.all_gather(direction, 'fsdp', axis=1, tiled=True)  34.7 us
  transfers between devices with their start and end apart: 2, of which 2 were waited for; matrix products, arithmetic and copies ran while one was open for 0% of the time, Pallas kernels for 0%

commit v1 on v0

v1 whole, which is shorter than its diff:
```python
import functools

import jax
import jax.numpy as jnp
from jax import lax
from jax.experimental import pallas as pl
from jax.experimental.pallas import tpu as pltpu
from jax.sharding import PartitionSpec as P

MESH = pl.DeviceIdType.MESH
LANES = 128
ROWS = 16
F32 = jnp.float32
BF16 = jnp.bfloat16
FAR, NEAR, LAST = 0, 1, 2


def kernel(
    sizes, acts, grad, basis, master, avg, avg_sq,
    new_master, weight, new_avg, new_avg_sq,
    part, rx, cross, ry, grad_v, grad_t, proj, local, from_core, held, ry2, rz2, full_dir,
    g_sem, x_send, x_recv, y_send, y_recv, c_send, c_recv, y2_send, y2_recv,
    z2_send, z2_recv, d_send, d_recv, y4_send, y4_recv, z4_send, z4_recv, s_send, s_recv,
):
    nz, ny, nc, nyh, nx = sizes
    groups = nyh * nx
    half_z = nz // 2
    dp, fs = lax.axis_index("dp"), lax.axis_index("fsdp")
    z, y, c = dp // (ny * nc), (dp // nc) % ny, dp % nc
    yh, x = fs // nx, fs % nx

    def dp_of(z_, y_, c_):
        return (z_ * ny + y_) * nc + c_

    def at_fsdp(f):
        return (dp, f)

    def at_dp(d):
        return (d, fs)

    def remote(src, dst, send, recv, device):
        return pltpu.make_async_remote_copy(
            src_ref=src, dst_ref=dst, send_sem=send, recv_sem=recv,
            device_id=device, device_id_type=MESH,
        )

    def wait_bytes(ref, sem):
        pltpu.make_async_copy(ref, ref, sem).wait()

    sibling = at_dp(dp_of(z, y, nc - 1 - c))

    barrier = pltpu.get_barrier_semaphore()

    def greet(device):
        pl.semaphore_signal(barrier, inc=1, device_id=device, device_id_type=MESH)

    @pl.loop(1, groups)
    def _(k):
        greet(at_fsdp((fs + k) % groups))

    @pl.loop(1, ny)
    def _(k):
        greet(at_dp(dp_of(z, (y + k) % ny, c)))

    @pl.loop(1, nz)
    def _(k):
        greet(at_dp(dp_of((z + k) % nz, y, c)))

    greet(sibling)

    load_grad = pltpu.make_async_copy(grad, grad_v, g_sem)
    load_grad.start()

    half_t = acts.shape[0] // 2

    def project(to_x, to_yh):
        columns = pl.ds(pl.multiple_of((to_yh * nx + to_x) * LANES, LANES), LANES)
        block = jnp.dot(acts[...], basis[:, columns], preferred_element_type=F32)
        part[to_x, to_yh, 0] = block[:half_t]
        part[to_x, to_yh, 1] = block[half_t:]

    def neighbour(way):
        return (x + 1) % nx if way == 0 else (x + nx - 1) % nx

    def x_copy(way, kind, to_yh, src):
        return remote(
            src, rx.at[way, kind, to_yh], x_send.at[way, kind, to_yh],
            x_recv.at[way, kind, to_yh], at_fsdp(yh * nx + neighbour(way)),
        )

    opposite = (x + 2) % nx
    for k in range(nyh):
        to_yh = (yh + 1 + k) % nyh
        project(opposite, to_yh)
        project(neighbour(0), to_yh)
        project(neighbour(1), to_yh)
        if k == 0:
            pl.semaphore_wait(barrier, groups - 1 + ny - 1 + nz - 1 + 1)
        for way in range(2):
            x_copy(way, FAR, to_yh, part.at[opposite, to_yh, way]).start()
        for way in range(2):
            x_copy(way, NEAR, to_yh, part.at[neighbour(way), to_yh, 1 - way]).start()
    for k in range(nyh):
        project(x, (yh + 1 + k) % nyh)

    def relay(to_yh):
        for way in range(2):
            copy = x_copy(way, LAST, to_yh, part.at[neighbour(way), to_yh, way])
            x_copy(way, FAR, to_yh, part.at[opposite, to_yh, way]).wait_recv()
            part[neighbour(way), to_yh, way] += rx[way, FAR, to_yh]
            copy.start()

    def x_total(to_yh, half):
        x_copy(1 - half, NEAR, to_yh, part.at[neighbour(0), to_yh, 0]).wait_recv()
        x_copy(half, LAST, to_yh, part.at[neighbour(0), to_yh, 0]).wait_recv()
        return part[x, to_yh, half] + rx[half, LAST, to_yh] + rx[1 - half, NEAR, to_yh]

    other_yh = (yh + 1) % nyh

    def y_copy(half):
        return remote(
            cross.at[half], ry.at[half], y_send.at[half], y_recv.at[half],
            at_fsdp(other_yh * nx + x),
        )

    relay(other_yh)
    relay(yh)

    load_grad.wait()
    wide = ny * nc * ROWS

    def turn(zz):
        columns = pl.ds(pl.multiple_of(zz * wide, wide), wide)
        turned = grad_v[:, columns].T
        for yy in range(ny):
            for cc in range(nc):
                lo = (yy * nc + cc) * ROWS
                grad_t[cc, yy, zz] = turned[lo : lo + ROWS]

    @pl.loop(0, nz // 2)
    def _(zz):
        turn(zz)

    for half in range(2):
        cross[half] = x_total(other_yh, half)
        y_copy(half).start()

    @pl.loop(nz // 2, nz)
    def _(zz):
        turn(zz)

    for half in range(2):
        total = x_total(yh, half)
        y_copy(half).wait_recv()
        proj[pl.ds(half * half_t, half_t)] = (total + ry[half]).astype(BF16)

    tokens = acts.shape[0]

    def term(cc, yy):
        rows = grad_t[cc, yy].reshape(nz * ROWS, tokens)
        block = jnp.dot(rows, proj[...], preferred_element_type=F32)
        local[cc, yy] = block.reshape(nz, ROWS, LANES)

    def core_copy(yy):
        return remote(
            local.at[nc - 1 - c, yy], from_core.at[yy], c_send.at[yy], c_recv.at[yy], sibling
        )

    @pl.loop(1, ny + 1)
    def _(k):
        yy = (y + k) % ny
        term(nc - 1 - c, yy)
        core_copy(yy).start()

    @pl.loop(1, ny + 1)
    def _(k):
        term(c, (y + k) % ny)

    def y2_copy(k):
        to_y = (y + k) % ny
        return remote(
            held.at[to_y], ry2.at[ny - k], y2_send.at[k], y2_recv.at[ny - k],
            at_dp(dp_of(z, to_y, c)),
        )

    def merge(k):
        yy = (y + k) % ny
        core_copy(yy).wait_recv()
        held[yy] = local[c, yy] + from_core[yy]

    @pl.loop(1, ny)
    def _(k):
        merge(k)
        y2_copy(k).start()

    merge(0)

    @pl.loop(1, ny)
    def _(k):
        y2_copy(ny - k).wait_recv()
        held[y] += ry2[k]

    def z2_copy(k):
        to_z = (z + k) % nz
        return remote(
            held.at[y, to_z], rz2.at[nz - k], z2_send.at[k], z2_recv.at[nz - k],
            at_dp(dp_of(to_z, y, c)),
        )

    @pl.loop(0, nz - 1)
    def _(i):
        z2_copy(half_z + (1 - 2 * (i % 2)) * ((i + 1) // 2)).start()

    proj_grad = held[y, z]
    for k in range(1, nz):
        z2_copy(nz - k).wait_recv()
        proj_grad = proj_grad + rz2[k]

    moment = 0.9 * avg[...] + 0.1 * proj_grad
    moment_sq = 0.95 * avg_sq[...] + 0.05 * proj_grad * proj_grad
    new_avg[...] = moment
    new_avg_sq[...] = moment_sq
    first_fix = 1.0 - 0.9**20
    second_fix = 1.0 - 0.95**20
    direction = moment / first_fix / (jnp.sqrt(moment_sq / second_fix) + 1e-08)

    def rank_block(f):
        return full_dir.at[:, pl.ds(pl.multiple_of(f * LANES, LANES), LANES)]

    rank_block(fs)[...] = direction.astype(BF16)

    def d_copy(k):
        return remote(
            rank_block(fs), rank_block(fs), d_send.at[k], d_recv.at[groups - k],
            at_fsdp((fs + k) % groups),
        )

    @pl.loop(1, groups)
    def _(k):
        d_copy(k).start()

    @pl.loop(1, groups)
    def _(k):
        remote(
            rank_block(fs), rank_block((fs + groups - k) % groups), d_send.at[k],
            d_recv.at[groups - k], at_fsdp((fs + k) % groups),
        ).wait_recv()

    tile = min(256, basis.shape[0])

    @pl.loop(0, basis.shape[0] // tile)
    def _(j):
        features = pl.ds(pl.multiple_of(j * tile, tile), tile)
        delta = lax.dot_general(
            full_dir[...], basis[features, :], (((1,), (1,)), ((), ())),
            preferred_element_type=F32,
        )
        updated = master[:, features] - 0.0125 * delta
        new_master[:, features] = updated
        weight[z, y, c, :, features] = updated.astype(BF16)

    def y4_copy(k):
        return remote(
            weight.at[z, y, c], weight.at[z, y, c], y4_send.at[k], y4_recv.at[ny - k],
            at_dp(dp_of(z, (y + k) % ny, c)),
        )

    def z4_copy(way, step, k):
        back = step - 1
        zz = (z + nz - back) % nz if way == 0 else (z + back) % nz
        to_z = (z + 1) % nz if way == 0 else (z + nz - 1) % nz
        block = weight.at[zz, (y + k) % ny, c]
        return remote(
            block, block, z4_send, z4_recv.at[way, step, k], at_dp(dp_of(to_z, y, c))
        )

    def share(zz, yy):
        block = weight.at[zz, yy, c]
        remote(block, block, s_send, s_recv, sibling).start()

    def last_way(k):
        return 0 if k < ny // 2 else 1

    @pl.loop(1, ny)
    def _(k):
        y4_copy(k).start()

    for k in range(ny):
        if k:
            y4_copy(ny - k).wait_recv()
        for way in range(2):
            if half_z > 1 or last_way(k) == way:
                z4_copy(way, 1, k).start()
        share(z, (y + k) % ny)

    @pl.loop(1, half_z)
    def _(step):
        for k in range(ny):
            for way in range(2):
                z4_copy(way, step, k).wait_recv()
                onward = z4_copy(way, step + 1, k)
                if last_way(k) == way:
                    onward.start()
                else:
                    pl.when(step < half_z - 1)(onward.start)
                share((z + nz - step) % nz if way == 0 else (z + step) % nz, (y + k) % ny)

    for k in range(ny):
        z4_copy(last_way(k), half_z, k).wait_recv()
        share((z + half_z) % nz, (y + k) % ny)

    for way in range(2):
        for kind in range(3):
            for to_yh in range(nyh):
                x_copy(way, kind, to_yh, part.at[0, 0, 0]).wait_send()
    for half in range(2):
        y_copy(half).wait_send()

    @pl.loop(0, ny)
    def _(k):
        core_copy(k).wait_send()

    @pl.loop(1, ny)
    def _(k):
        y2_copy(k).wait_send()
        y4_copy(k).wait_send()

    @pl.loop(1, nz)
    def _(k):
        z2_copy(k).wait_send()

    @pl.loop(1, groups)
    def _(k):
        d_copy(k).wait_send()

    wait_bytes(weight.at[pl.ds(0, nz - 1), :, 0], z4_send)
    wait_bytes(weight.at[:, :, c], s_send)
    wait_bytes(weight.at[:, :, nc - 1 - c], s_recv)


def on_device(sizes, acts, grad_out, basis, master, exp_avg, exp_avg_sq):
    nz, ny, nc, nyh, nx = sizes
    tokens, wide = acts.shape
    groups = nyh * nx
    dma = pltpu.SemaphoreType.DMA
    vmem = pl.BlockSpec(memory_space=pltpu.VMEM)
    shape = jax.ShapeDtypeStruct
    half = tokens // 2
    new_master, weight, new_avg, new_avg_sq = pl.pallas_call(
        functools.partial(kernel, sizes),
        out_shape=(
            shape((ROWS, wide), F32),
            shape((nz, ny, nc, ROWS, wide), BF16),
            shape((ROWS, LANES), F32),
            shape((ROWS, LANES), F32),
        ),
        in_specs=[vmem, pl.BlockSpec(memory_space=pl.ANY), vmem, vmem, vmem, vmem],
        out_specs=[vmem] * 4,
        scratch_shapes=[
            pltpu.VMEM((nx, nyh, 2, half, LANES), F32),
            pltpu.VMEM((2, 3, nyh, half, LANES), F32),
            pltpu.VMEM((2, half, LANES), F32),
            pltpu.VMEM((2, half, LANES), F32),
            pltpu.VMEM(grad_out.shape, BF16),
            pltpu.VMEM((nc, ny, nz, ROWS, tokens), BF16),
            pltpu.VMEM((tokens, LANES), BF16),
            pltpu.VMEM((nc, ny, nz, ROWS, LANES), F32),
            pltpu.VMEM((ny, nz, ROWS, LANES), F32),
            pltpu.VMEM((ny, nz, ROWS, LANES), F32),
            pltpu.VMEM((ny, nz, ROWS, LANES), F32),
            pltpu.VMEM((nz, ROWS, LANES), F32),
            pltpu.VMEM((ROWS, groups * LANES), BF16),
            dma,
            dma((2, 3, nyh)), dma((2, 3, nyh)),
            dma((2,)), dma((2,)),
            dma((ny,)), dma((ny,)),
            dma((ny,)), dma((ny,)),
            dma((nz,)), dma((nz,)),
            dma((groups,)), dma((groups,)),
            dma((ny,)), dma((ny,)),
            dma, dma((2, nz // 2 + 1, ny)),
            dma, dma,
        ],
        compiler_params=pltpu.CompilerParams(
            collective_id=0, has_side_effects=True, vmem_limit_bytes=48 * 1024 * 1024
        ),
        cost_estimate=pl.CostEstimate(
            flops=2 * tokens * LANES * (groups * wide + nz * ny * nc * ROWS),
            bytes_accessed=16 * 1024 * 1024,
            transcendentals=ROWS * LANES,
        ),
        name="galore_step",
    )(acts, grad_out, basis, master, exp_avg, exp_avg_sq)
    return new_master, weight.reshape(nz * ny * nc * ROWS, wide), new_avg, new_avg_sq


def build(mesh, sizes):
    return jax.shard_map(
        functools.partial(on_device, sizes),
        mesh=mesh,
        in_specs=(
            P("dp", "fsdp"),
            P("dp", None),
            P("fsdp", None),
            P("dp", "fsdp"),
            P("dp", "fsdp"),
            P("dp", "fsdp"),
        ),
        out_specs=(P("dp", "fsdp"), P(None, "fsdp"), P("dp", "fsdp"), P("dp", "fsdp")),
        check_vma=False,
    )


def solution(mesh):
    return build(mesh, (16, 4, 2, 2, 4))
```

time: 964 us -> 126 us (0.13)
  waiting for transfers between devices: 790 us -> 0 us
  blocking collectives: 144 us -> 0 us
  Pallas kernels: 0 us -> 112 us
  between operations: 14.1 us -> 0.66 us
    reduce_scatter x1 -> x0, waiting for transfers between devices: 561 us -> none  [on_device(): lax.psum_scatter(local_grad, 'dp', scatter_dimension=0, tiled=True)]
    all_gather x1 -> x0, waiting for transfers between devices: 230 us -> none  [on_device(): lax.all_gather(new_master.astype(jnp.bfloat16), 'dp', axis=0, tiled=True)]
    pallas_call x0 -> x1, Pallas kernels: none -> 112 us  [on_device(): pl.pallas_call(functools.partial(kernel, sizes), out_shape=(shape((ROWS,...]
    psum x1 -> x0, blocking collectives: 109 us -> none  [on_device(): summed = lax.psum(partial_sum, 'fsdp')]
    all_gather x1 -> x0, blocking collectives: 34.7 us -> none  [on_device(): full_direction = lax.all_gather(direction, 'fsdp', axis=1, tiled=True)]
  transfers between devices with their start and end apart: 2 -> 0, of which waited for: 2 -> 0; matrix products, arithmetic and copies ran while one was open for 0% -> 0% of each run, Pallas kernels for 0% -> 0%
where the time goes in v1:
time: 126 us; the launch traced here: 125 us
  Pallas kernels  112 us (89%)
  local copies, waits for them, and re-layouts  12.8 us (10%)
    pallas_call x1, Pallas kernels, on_device(): pl.pallas_call(functools.partial(kernel, sizes), out_shape=(shape((ROWS,...  112 us
    unnamed x16, local copies, waits for them, and re-layouts  12.8 us

profile of v1, /device:TPU:1, one launch (start us, length us, event | category | flops | bytes accessed | tf_op | source)
XLA Modules:
  0.0 125.3 jit_solution(16693991798458723951)
XLA Ops:
  0.6 0.0 copy-start
  0.6 1.6 %copy-done = bf16[1024,1024]{1,0:T(8,128)(2,1)S(1)} copy-done((bf16[1024,1024]{1,0:T(8,128)(2,1)S(1)}, bf16[1024,1024]{1,0:T(8,128)(2,1)}, u32[]{:S(2)}) %copy-start) | copy-done | bytes 2097176
  2.2 0.0 copy-start.1
  2.2 1.4 %copy-done.1 = bf16[384,2048]{1,0:T(8,128)(2,1)S(1)} copy-done((bf16[384,2048]{1,0:T(8,128)(2,1)S(1)}, bf16[384,2048]{1,0:T(8,128)(2,1)}, u32[]{:S(2)}) %copy-start.1) | copy-done | bytes 1572888
  3.6 0.0 copy-start.2
  3.6 1.1 copy-done.2
  4.8 0.0 copy-start.3
  4.8 0.8 copy-done.3
  5.6 0.0 copy-start.4
  5.6 0.7 copy-done.4
  6.3 0.0 copy-start.5
  6.3 0.7 copy-done.5
  7.0 111.9 %galore_step.1 = (f32[16,1024]{1,0:T(8,128)S(1)}, bf16[16,4,2,16,1024]{4,3,2,1,0:T(8,128)(2,1)}, f32[16,128]{1,0:T(8,128)S(1)}, f32[16,128]{1,0:T(8,128)S(1)}) custom-call(bf16[384,1024]{1,0:T(8,128)(2,1)S(1)} %copy-done.2, bf16[384,2048]{1,0:T(8,128)(2,1)S(1)} %copy-done.1, bf16[1024,1024]{1,0:T(8,128)(2,1)S(1)} %copy-done, f32[16,1024]{1,0:T(8,128)S(1)} %copy-done.3, ...), custom_call_target="tpu_custom_call" | custom-call | flops 1006632960 | bytes 16777216 | tf_op jit(solution)/shard_map/galore_step/pallas_call | solution.py:349
  118.9 0.6 copy.14
  119.5 4.6 %copy.15 = bf16[2048,1024]{1,0:T(8,128)(2,1)} copy(bf16[2048,1024]{1,0:T(8,128)(2,1)} %bitcast.1) | data formatting | bytes 8388608
  124.1 0.6 copy.16
  124.7 0.6 copy.17
Async XLA Ops:
  0.6 1.6 %copy-start = (bf16[1024,1024]{1,0:T(8,128)(2,1)S(1)}, bf16[1024,1024]{1,0:T(8,128)(2,1)}, u32[]{:S(2)}) copy-start(bf16[1024,1024]{1,0:T(8,128)(2,1)} %basis.1) | copy-start | bytes 6291460
  2.2 1.4 %copy-start.1 = (bf16[384,2048]{1,0:T(8,128)(2,1)S(1)}, bf16[384,2048]{1,0:T(8,128)(2,1)}, u32[]{:S(2)}) copy-start(bf16[384,2048]{1,0:T(8,128)(2,1)} %grad.1) | copy-start | bytes 4718596
  3.6 1.1 copy-start.2
  4.8 0.8 copy-start.3
  5.6 0.7 copy-start.4
  6.3 0.7 copy-start.5

commit v2 on v1

v2 whole, which is shorter than its diff:
```python
import functools

import jax
import jax.numpy as jnp
from jax import lax
from jax.experimental import pallas as pl
from jax.experimental.pallas import tpu as pltpu
from jax.sharding import PartitionSpec as P

MESH = pl.DeviceIdType.MESH
LANES = 128
ROWS = 16
F32 = jnp.float32
BF16 = jnp.bfloat16
FAR, NEAR, LAST = 0, 1, 2


def kernel(
    sizes, acts_h, grad, basis_h, master_h, avg_h, avg_sq_h,
    new_master, weight_h, new_avg, new_avg_sq,
    weight, acts, basis, master, avg, avg_sq, part, rx, cross, mid, ry, grad_v, grad_t, proj, local, from_core,
    held_a, held_b, rya, rza, rzb, ryb, basis_t, full_dir,
    in_sems, x_send, x_recv, m_send, m_recv, y_send, y_recv, c_send, c_recv, ya_send, ya_recv,
    za_send, za_recv, zb_send, zb_recv, yb_send, yb_recv, d_send, d_recv, y4_send, y4_recv, z4_send, z4_recv, s_send, s_recv, w_sem,
    b_send, b_recv, by_send, by_recv, t_send, t_recv, v_sem,
):
    nz, ny, nc, nyh, nx = sizes
    groups = nyh * nx
    half_z = nz // 2
    dp, fs = lax.axis_index("dp"), lax.axis_index("fsdp")
    z, y, c = dp // (ny * nc), (dp // nc) % ny, dp % nc
    yh, x = fs // nx, fs % nx

    def dp_of(z_, y_, c_):
        return (z_ * ny + y_) * nc + c_

    def at_fsdp(f):
        return (dp, f)

    def at_dp(d):
        return (d, fs)

    def remote(src, dst, send, recv, device):
        return pltpu.make_async_remote_copy(
            src_ref=src, dst_ref=dst, send_sem=send, recv_sem=recv,
            device_id=device, device_id_type=MESH,
        )

    def wait_bytes(ref, sem):
        pltpu.make_async_copy(ref, ref, sem).wait()

    sibling = at_dp(dp_of(z, y, nc - 1 - c))

    loads = [
        pltpu.make_async_copy(src, dst, in_sems.at[i])
        for i, (src, dst) in enumerate(
            ((acts_h, acts), (basis_h, basis), (grad, grad_v), (master_h, master),
             (avg_h, avg), (avg_sq_h, avg_sq))
        )
    ]
    for load in loads:
        load.start()

    barrier = pltpu.get_barrier_semaphore()

    def greet(device):
        pl.semaphore_signal(barrier, inc=1, device_id=device, device_id_type=MESH)

    @pl.loop(1, groups)
    def _(k):
        greet(at_fsdp((fs + k) % groups))

    @pl.loop(1, ny)
    def _(k):
        greet(at_dp(dp_of(z, (y + k) % ny, c)))

    @pl.loop(1, nz)
    def _(k):
        greet(at_dp(dp_of((z + k) % nz, y, c)))

    line = yh * ny + y
    hop = ny // 2

    def along_y(way):
        there = (line + (hop if way == 0 else nyh * ny - hop)) % (nyh * ny)
        return (dp_of(z, there % ny, c), (there // ny) * nx + x)

    greet(sibling)
    for way in range(2):
        greet(along_y(way))


    quarter = acts.shape[0] // 4
    loads[0].wait()
    loads[1].wait()

    def project(to_x, to_yh):
        columns = pl.ds(pl.multiple_of((to_yh * nx + to_x) * LANES, LANES), LANES)
        block = jnp.dot(acts[...], basis[:, columns], preferred_element_type=F32)
        part[to_x, to_yh] = block.reshape(2, 2, quarter, LANES)

    def neighbour(way):
        return (x + 1) % nx if way == 0 else (x + nx - 1) % nx

    opposite = (x + 2) % nx
    other_yh = (yh + 1) % nyh

    def x_copy(way, kind, to_yh, piece):
        to_x = opposite if kind == FAR else neighbour(way)
        half = 1 - way if kind == NEAR else way
        return remote(
            part.at[to_x, to_yh, half, piece], rx.at[way, kind, to_yh, piece],
            x_send.at[way, kind, to_yh, piece], x_recv.at[way, kind, to_yh, piece],
            at_fsdp(yh * nx + neighbour(way)),
        )

    def send_first(to_yh):
        for kind in (FAR, NEAR):
            for piece in range(2):
                for way in range(2):
                    x_copy(way, kind, to_yh, piece).start()

    def send_last(to_yh):
        for piece in range(2):
            for way in range(2):
                x_copy(way, FAR, to_yh, piece).wait_recv()
                part[neighbour(way), to_yh, way, piece] += rx[way, FAR, to_yh, piece]
                x_copy(way, LAST, to_yh, piece).start()

    def x_total(to_yh, half, piece):
        x_copy(1 - half, NEAR, to_yh, piece).wait_recv()
        x_copy(half, LAST, to_yh, piece).wait_recv()
        return (
            part[x, to_yh, half, piece]
            + rx[half, LAST, to_yh, piece]
            + rx[1 - half, NEAR, to_yh, piece]
        )

    def m_copy(half, piece):
        return remote(
            cross.at[half, piece], mid.at[half, piece], m_send.at[half, piece],
            m_recv.at[half, piece], along_y(half),
        )

    def y_copy(half, piece):
        return remote(
            mid.at[half, piece], ry.at[half, piece], y_send.at[half, piece],
            y_recv.at[half, piece], along_y(half),
        )

    wide = ny * nc * ROWS

    def turn(first, last):
        @pl.loop(first, last)
        def _(zz):
            columns = pl.ds(pl.multiple_of(zz * wide, wide), wide)
            turned = grad_v[:, columns].T
            for yy in range(ny):
                for cc in range(nc):
                    lo = (yy * nc + cc) * ROWS
                    grad_t[cc, yy, zz] = turned[lo : lo + ROWS]

    project(opposite, other_yh)
    project(neighbour(0), other_yh)
    project(neighbour(1), other_yh)
    pl.semaphore_wait(barrier, groups - 1 + ny - 1 + nz - 1 + 1 + 2)
    send_first(other_yh)
    project(x, other_yh)
    send_last(other_yh)
    project(opposite, yh)
    project(neighbour(0), yh)
    project(neighbour(1), yh)
    send_first(yh)
    project(x, yh)
    for piece in range(2):
        for half in range(2):
            cross[half, piece] = x_total(other_yh, half, piece)
            m_copy(half, piece).start()
    send_last(yh)
    loads[2].wait()
    turn(0, nz // 2)
    for piece in range(2):
        for half in range(2):
            m_copy(half, piece).wait_recv()
            y_copy(half, piece).start()
    turn(nz // 2, nz)
    for piece in range(2):
        for half in range(2):
            total = x_total(yh, half, piece)
            y_copy(half, piece).wait_recv()
            rows = pl.ds((2 * half + piece) * quarter, quarter)
            proj[rows] = (total + ry[half, piece]).astype(BF16)
    for load in loads[3:]:
        load.wait()

    tokens = acts.shape[0]

    def term(cc, yy):
        rows = grad_t[cc, yy].reshape(nz * ROWS, tokens)
        block = jnp.dot(rows, proj[...], preferred_element_type=F32)
        local[cc, yy] = block.reshape(nz, ROWS, LANES)

    def core_copy(yy):
        return remote(
            local.at[nc - 1 - c, yy], from_core.at[yy], c_send.at[yy], c_recv.at[yy], sibling
        )

    @pl.loop(1, ny + 1)
    def _(k):
        yy = (y + k) % ny
        term(nc - 1 - c, yy)
        core_copy(yy).start()

    @pl.loop(1, ny + 1)
    def _(k):
        term(c, (y + k) % ny)

    low = ROWS // 2

    def to_y(k):
        return at_dp(dp_of(z, (y + k) % ny, c))

    def to_z(k):
        return at_dp(dp_of((z + k) % nz, y, c))

    def ya_copy(k):
        return remote(
            held_a.at[(y + k) % ny], rya.at[ny - k], ya_send.at[k], ya_recv.at[ny - k], to_y(k)
        )

    def za_copy(k):
        return remote(
            held_a.at[y, (z + k) % nz], rza.at[nz - k], za_send.at[k], za_recv.at[nz - k], to_z(k)
        )

    def zb_copy(k):
        return remote(
            held_b.at[(z + k) % nz], rzb.at[nz - k], zb_send.at[k], zb_recv.at[nz - k], to_z(k)
        )

    def yb_copy(k):
        return remote(
            held_b.at[z, (y + k) % ny], ryb.at[ny - k], yb_send.at[k], yb_recv.at[ny - k], to_y(k)
        )

    def merge(k):
        yy = (y + k) % ny
        core_copy(yy).wait_recv()
        merged = local[c, yy] + from_core[yy]
        held_a[yy] = merged[:, :low]
        held_b[:, yy] = merged[:, low:]

    def far_first(i):
        return half_z + (1 - 2 * (i % 2)) * ((i + 1) // 2)

    @pl.loop(1, ny)
    def _(k):
        merge(k)
        ya_copy(k).start()

    merge(0)

    @pl.loop(0, nz - 1)
    def _(i):
        zb_copy(far_first(i)).start()

    @pl.loop(1, ny)
    def _(k):
        ya_copy(ny - k).wait_recv()
        held_a[y] += rya[k]

    @pl.loop(0, nz - 1)
    def _(i):
        za_copy(far_first(i)).start()

    @pl.loop(0, basis.shape[0] // LANES)
    def _(j):
        features = pl.ds(pl.multiple_of(j * LANES, LANES), LANES)
        basis_t[:, features] = basis[features, :].T

    @pl.loop(1, nz)
    def _(k):
        zb_copy(nz - k).wait_recv()
        held_b[z] += rzb[k]

    @pl.loop(1, ny)
    def _(k):
        yb_copy(k).start()

    grad_a, grad_b = held_a[y, z], held_b[z, y]
    for k in range(1, nz):
        za_copy(nz - k).wait_recv()
        grad_a = grad_a + rza[k]
    for k in range(1, ny):
        yb_copy(ny - k).wait_recv()
        grad_b = grad_b + ryb[k]
    proj_grad = jnp.concatenate([grad_a, grad_b], axis=0)

    moment = 0.9 * avg[...] + 0.1 * proj_grad
    moment_sq = 0.95 * avg_sq[...] + 0.05 * proj_grad * proj_grad
    new_avg[...] = moment
    new_avg_sq[...] = moment_sq
    first_fix = 1.0 - 0.9**20
    second_fix = 1.0 - 0.95**20
    direction = moment / first_fix / (jnp.sqrt(moment_sq / second_fix) + 1e-08)

    def rank_block(f):
        return full_dir.at[:, pl.ds(pl.multiple_of(f * LANES, LANES), LANES)]

    rank_block(fs)[...] = direction.astype(BF16)

    def d_copy(k):
        return remote(
            rank_block(fs), rank_block(fs), d_send.at[k], d_recv.at[groups - k],
            at_fsdp((fs + k) % groups),
        )

    @pl.loop(1, groups)
    def _(k):
        d_copy(k).start()

    @pl.loop(1, groups)
    def _(k):
        remote(
            rank_block(fs), rank_block((fs + groups - k) % groups), d_send.at[k],
            d_recv.at[groups - k], at_fsdp((fs + k) % groups),
        ).wait_recv()

    tile = basis.shape[0] // 4
    first = pl.ds(0, 3 * tile)
    second = pl.ds(3 * tile, tile)

    def update(j):
        features = pl.ds(pl.multiple_of(j * tile, tile), tile)
        delta = jnp.dot(full_dir[...], basis_t[:, features], preferred_element_type=F32)
        updated = master[:, features] - 0.0125 * delta
        new_master[:, features] = updated
        weight[z, y, c, :, features] = updated.astype(BF16)

    def y4_copy(k):
        block = weight.at[z, y, c, :, first]
        return remote(
            block, block, y4_send.at[k], y4_recv.at[ny - k], at_dp(dp_of(z, (y + k) % ny, c))
        )

    def behind(way, step):
        return (z + nz - step) % nz if way == 0 else (z + step) % nz

    def z4_copy(way, stage, ahead, k):
        block = weight.at[behind(way, 2 * (stage - 1)), (y + k) % ny, c, :, first]
        return remote(
            block, block, z4_send, z4_recv.at[way, 2 * (stage - 1) + ahead, k],
            at_dp(dp_of(behind(1 - way, ahead), y, c)),
        )

    def z4_wait(way, step, k):
        wait_bytes(
            weight.at[behind(way, step), (y + k) % ny, c, :, first], z4_recv.at[way, step, k]
        )

    def b_copy(way, stage, ahead):
        block = weight.at[behind(way, 2 * (stage - 1)), y, c, :, second]
        return remote(
            block, block, b_send, b_recv.at[way, 2 * (stage - 1) + ahead],
            at_dp(dp_of(behind(1 - way, ahead), y, c)),
        )

    def b_wait(way, step):
        wait_bytes(weight.at[behind(way, step), y, c, :, second], b_recv.at[way, step])

    def spread(zz):
        block = weight.at[zz, y, c, :, second]

        @pl.loop(1, ny)
        def _(k):
            remote(
                block, block, by_send, by_recv.at[ny - k], at_dp(dp_of(z, (y + k) % ny, c))
            ).start()

    def share(zz):
        block = weight.at[zz, :, c, :, first]
        remote(block, block, s_send, s_recv.at[zz], sibling).start()

    def share_line(yy):
        block = weight.at[:, yy, c, :, second]
        remote(block, block, t_send, t_recv.at[yy], sibling).start()

    def store(zz):
        wait_bytes(weight.at[zz, :, nc - 1 - c, :, first], s_recv.at[zz])
        pltpu.make_async_copy(
            weight.at[zz, :, :, :, first], weight_h.at[zz, :, :, :, first], w_sem
        ).start()

    def store_line(yy):
        wait_bytes(weight.at[:, yy, nc - 1 - c, :, second], t_recv.at[yy])
        pltpu.make_async_copy(
            weight.at[:, yy, :, :, second], weight_h.at[:, yy, :, :, second], v_sem
        ).start()

    def last_way(k):
        return 0 if k < ny // 2 else 1

    stages = half_z // 2

    def onward(way, stage, copy, chosen):
        if chosen:
            copy(way, stage, 2).start()
        else:
            pl.when(stage < stages)(lambda: copy(way, stage, 2).start())
        copy(way, stage, 1).start()

    def z4_onward(way, stage, k):
        onward(way, stage, lambda *args: z4_copy(*args, k), last_way(k) == way)

    update(3)
    for way in range(2):
        onward(way, jnp.int32(1), b_copy, way == 0)
    spread(z)
    pl.loop(0, 3)(update)
    for k in range(ny):
        if k:
            y4_copy(ny - k).wait_recv()
        for way in range(2):
            z4_onward(way, jnp.int32(1), k)
        if not k:
            for j in range(1, ny):
                y4_copy(j).start()
    share(z)

    @pl.loop(1, stages)
    def _(stage):
        for way in range(2):
            b_wait(way, 2 * stage)
            onward(way, stage + 1, b_copy, way == 0)
        for k in range(ny):
            for way in range(2):
                z4_wait(way, 2 * stage, k)
                z4_onward(way, stage + 1, k)
        for way in range(2):
            b_wait(way, 2 * stage - 1)
            for k in range(ny):
                z4_wait(way, 2 * stage - 1, k)
            for back in range(2):
                spread(behind(way, 2 * stage - back))
                share(behind(way, 2 * stage - back))

        @pl.when(stage > 1)
        def _():
            for way in range(2):
                for back in range(2, 4):
                    store(behind(way, 2 * stage - back))

    for way in range(2):
        b_wait(way, half_z - 1)
        spread(behind(way, half_z - 1))
    b_wait(0, half_z)
    spread(behind(0, half_z))
    share_line(y)
    for way in range(2):
        for k in range(ny):
            z4_wait(way, half_z - 1, k)
        share(behind(way, half_z - 1))
    for k in range(ny):
        z4_wait(last_way(k), half_z, k)
    share(behind(0, half_z))
    store(z)
    for way in range(2):
        for step in range(max(half_z - 3, 1), half_z):
            store(behind(way, step))
    for k in range(1, ny):
        yy = (y + k) % ny
        wait_bytes(weight.at[:, yy, c, :, second], by_recv.at[k])
        share_line(yy)
    store(behind(0, half_z))
    for k in range(ny):
        store_line((y + k) % ny)

    for way in range(2):
        for kind in range(3):
            for to_yh in range(nyh):
                for piece in range(2):
                    x_copy(way, kind, to_yh, piece).wait_send()
    for half in range(2):
        for piece in range(2):
            m_copy(half, piece).wait_send()
            y_copy(half, piece).wait_send()

    @pl.loop(0, ny)
    def _(k):
        core_copy(k).wait_send()

    @pl.loop(1, ny)
    def _(k):
        ya_copy(k).wait_send()
        yb_copy(k).wait_send()
        y4_copy(k).wait_send()

    @pl.loop(1, nz)
    def _(k):
        za_copy(k).wait_send()
        zb_copy(k).wait_send()

    @pl.loop(1, groups)
    def _(k):
        d_copy(k).wait_send()

    wait_bytes(weight.at[pl.ds(0, nz - 1), :, 0, :, first], z4_send)
    wait_bytes(weight.at[pl.ds(0, nz - 1), 0, 0, :, second], b_send)
    wait_bytes(weight.at[:, pl.ds(0, ny - 1), 0, :, second], by_send)
    wait_bytes(weight.at[:, :, 0, :, first], s_send)
    wait_bytes(weight.at[:, :, 0, :, second], t_send)
    wait_bytes(weight.at[:, :, :, :, first], w_sem)
    wait_bytes(weight.at[:, :, :, :, second], v_sem)


def deliver(master, weight, avg, avg_sq, *refs):
    outs, (staged, *small, sems) = refs[:4], refs[4:]
    moves = [(master, small[0], outs[0]), (avg, small[1], outs[2]), (avg_sq, small[2], outs[3])]
    moves += [(weight.at[i], staged.at[i], outs[1].at[i]) for i in range(weight.shape[0])]
    reads = [pltpu.make_async_copy(m[0], m[1], sems.at[0, i]) for i, m in enumerate(moves)]
    writes = [pltpu.make_async_copy(m[1], m[2], sems.at[1, i]) for i, m in enumerate(moves)]
    for read in reads:
        read.start()
    for read, write in zip(reads, writes):
        read.wait()
        write.start()
    for write in writes:
        write.wait()


def on_device(sizes, acts, grad_out, basis, master, exp_avg, exp_avg_sq):
    nz, ny, nc, nyh, nx = sizes
    tokens, wide = acts.shape
    groups = nyh * nx
    dma = pltpu.SemaphoreType.DMA
    vmem = pl.BlockSpec(memory_space=pltpu.VMEM)
    hbm = pl.BlockSpec(memory_space=pltpu.HBM)
    shape = jax.ShapeDtypeStruct
    quarter = tokens // 4
    results = pl.pallas_call(
        functools.partial(kernel, sizes),
        out_shape=(
            shape((ROWS, wide), F32),
            shape((nz, ny, nc, ROWS, wide), BF16),
            shape((ROWS, LANES), F32),
            shape((ROWS, LANES), F32),
        ),
        in_specs=[hbm] * 6,
        out_specs=[vmem, hbm, vmem, vmem],
        scratch_shapes=[
            pltpu.VMEM((nz, ny, nc, ROWS, wide), BF16),
            pltpu.VMEM(acts.shape, BF16),
            pltpu.VMEM(basis.shape, BF16),
            pltpu.VMEM(master.shape, F32),
            pltpu.VMEM(exp_avg.shape, F32),
            pltpu.VMEM(exp_avg_sq.shape, F32),
            pltpu.VMEM((nx, nyh, 2, 2, quarter, LANES), F32),
            pltpu.VMEM((2, 3, nyh, 2, quarter, LANES), F32),
            pltpu.VMEM((2, 2, quarter, LANES), F32),
            pltpu.VMEM((2, 2, quarter, LANES), F32),
            pltpu.VMEM((2, 2, quarter, LANES), F32),
            pltpu.VMEM(grad_out.shape, BF16),
            pltpu.VMEM((nc, ny, nz, ROWS, tokens), BF16),
            pltpu.VMEM((tokens, LANES), BF16),
            pltpu.VMEM((nc, ny, nz, ROWS, LANES), F32),
            pltpu.VMEM((ny, nz, ROWS, LANES), F32),
            pltpu.VMEM((ny, nz, ROWS // 2, LANES), F32),
            pltpu.VMEM((nz, ny, ROWS // 2, LANES), F32),
            pltpu.VMEM((ny, nz, ROWS // 2, LANES), F32),
            pltpu.VMEM((nz, ROWS // 2, LANES), F32),
            pltpu.VMEM((nz, ny, ROWS // 2, LANES), F32),
            pltpu.VMEM((ny, ROWS // 2, LANES), F32),
            pltpu.VMEM((groups * LANES, wide), BF16),
            pltpu.VMEM((ROWS, groups * LANES), BF16),
            dma((6,)),
            dma((2, 3, nyh, 2)), dma((2, 3, nyh, 2)),
            dma((2, 2)), dma((2, 2)),
            dma((2, 2)), dma((2, 2)),
            dma((ny,)), dma((ny,)),
            dma((ny,)), dma((ny,)),
            dma((nz,)), dma((nz,)),
            dma((nz,)), dma((nz,)),
            dma((ny,)), dma((ny,)),
            dma((groups,)), dma((groups,)),
            dma((ny,)), dma((ny,)),
            dma, dma((2, nz // 2 + 1, ny)),
            dma, dma((nz,)), dma,
            dma, dma((2, nz // 2 + 1)), dma, dma((ny,)), dma, dma((ny,)), dma,
        ],
        compiler_params=pltpu.CompilerParams(
            collective_id=0, has_side_effects=True, vmem_limit_bytes=58 * 1024 * 1024
        ),
        cost_estimate=pl.CostEstimate(
            flops=2 * tokens * LANES * (groups * wide + nz * ny * nc * ROWS),
            bytes_accessed=16 * 1024 * 1024,
            transcendentals=ROWS * LANES,
        ),
        name="galore_step",
    )(acts, grad_out, basis, master, exp_avg, exp_avg_sq)
    new_master, weight, new_avg, new_avg_sq = pl.pallas_call(
        deliver,
        out_shape=[shape(r.shape, r.dtype) for r in results],
        in_specs=[hbm] * 4,
        out_specs=[hbm] * 4,
        scratch_shapes=[pltpu.VMEM(results[i].shape, results[i].dtype) for i in (1, 0, 2, 3)]
        + [dma((2, 3 + nz))],
        compiler_params=pltpu.CompilerParams(vmem_limit_bytes=58 * 1024 * 1024),
        name="deliver",
    )(*results)
    return new_master, weight.reshape(nz * ny * nc * ROWS, wide), new_avg, new_avg_sq


def build(mesh, sizes):
    return jax.shard_map(
        functools.partial(on_device, sizes),
        mesh=mesh,
        in_specs=(
            P("dp", "fsdp"),
            P("dp", None),
            P("fsdp", None),
            P("dp", "fsdp"),
            P("dp", "fsdp"),
            P("dp", "fsdp"),
        ),
        out_specs=(P("dp", "fsdp"), P(None, "fsdp"), P("dp", "fsdp"), P("dp", "fsdp")),
        check_vma=False,
    )


def solution(mesh):
    return build(mesh, (16, 4, 2, 2, 4))
```

time: 126 us -> 112 us (0.89)
  local copies, waits for them, and re-layouts: 12.8 us -> 0 us
    unnamed x16 -> x0, local copies, waits for them, and re-layouts: 12.8 us -> none
    pallas_call x1, Pallas kernels: 112 us -> 108 us  [on_device(): pl.pallas_call(functools.partial(kernel, sizes), out_shape=(shape((ROWS,...]
    pallas_call x0 -> x1, Pallas kernels: none -> 4.05 us  [on_device(): pl.pallas_call(deliver, out_shape=[shape(r.shape, r.dtype) for r in resul...]
where the time goes in v2:
time: 112 us
  Pallas kernels  112 us (100%)
    pallas_call x1, Pallas kernels, on_device(): pl.pallas_call(functools.partial(kernel, sizes), out_shape=(shape((ROWS,...  108 us
    pallas_call x1, Pallas kernels, on_device(): pl.pallas_call(deliver, out_shape=[shape(r.shape, r.dtype) for r in resul...  4.05 us

profile of v2, /device:TPU:1, one launch (start us, length us, event | category | flops | bytes accessed | tf_op | source)
XLA Modules:
  0.0 112.3 jit_solution(3299502208130231169)
XLA Ops:
  0.6 107.6 %galore_step.1 = (f32[16,1024]{1,0:T(8,128)}, bf16[16,4,2,16,1024]{4,3,2,1,0:T(8,128)(2,1)}, f32[16,128]{1,0:T(8,128)}, f32[16,128]{1,0:T(8,128)}) custom-call(bf16[384,1024]{1,0:T(8,128)(2,1)} %acts_h.1, bf16[384,2048]{1,0:T(8,128)(2,1)} %grad.1, bf16[1024,1024]{1,0:T(8,128)(2,1)} %basis_h.1, f32[16,1024]{1,0:T(8,128)} %master_h.1, f32[16,128]{1,0:T(8,128)} %avg_h.1, ...), custom_call_target="tpu_custom_call" | custom-call | flops 1006632960 | bytes 16777216 | tf_op jit(solution)/shard_map/galore_step/pallas_call | solution.py:540
  108.3 4.1 %deliver.1 = (f32[16,1024]{1,0:T(8,128)}, bf16[16,4,2,16,1024]{4,3,2,1,0:T(8,128)(2,1)}, f32[16,128]{1,0:T(8,128)}, f32[16,128]{1,0:T(8,128)}) custom-call(f32[16,1024]{1,0:T(8,128)} %get-tuple-element.12.master, bf16[16,4,2,16,1024]{4,3,2,1,0:T(8,128)(2,1)} %get-tuple-element.13.weight, f32[16,128]{1,0:T(8,128)} %get-tuple-element.14.avg, ...), custom_call_target="tpu_custom_call" | custom-call | tf_op jit(solution)/shard_map/deliver/pallas_call | solution.py:600

commit v3 on v2

--- a/solution.py
+++ b/solution.py
@@ -13,14 +13,15 @@
 F32 = jnp.float32
 BF16 = jnp.bfloat16
 FAR, NEAR, LAST = 0, 1, 2
+FIRST_HOPS = (2, 1, 2, 1, 2)
 
 
 def kernel(
     sizes, acts_h, grad, basis_h, master_h, avg_h, avg_sq_h,
     new_master, weight_h, new_avg, new_avg_sq,
-    weight, acts, basis, master, avg, avg_sq, part, rx, cross, mid, ry, grad_v, grad_t, proj, local, from_core,
+    weight, acts, basis, master, avg, avg_sq, part, rx, cross, ry, grad_v, grad_t, proj, local, from_core,
     held_a, held_b, rya, rza, rzb, ryb, basis_t, full_dir,
-    in_sems, x_send, x_recv, m_send, m_recv, y_send, y_recv, c_send, c_recv, ya_send, ya_recv,
+    in_sems, x_send, x_recv, y_send, y_recv, c_send, c_recv, ya_send, ya_recv,
     za_send, za_recv, zb_send, zb_recv, yb_send, yb_recv, d_send, d_recv, y4_send, y4_recv, z4_send, z4_recv, s_send, s_recv, w_sem,
     b_send, b_recv, by_send, by_recv, t_send, t_recv, v_sem,
 ):
@@ -78,16 +79,7 @@
     def _(k):
         greet(at_dp(dp_of((z + k) % nz, y, c)))
 
-    line = yh * ny + y
-    hop = ny // 2
-
-    def along_y(way):
-        there = (line + (hop if way == 0 else nyh * ny - hop)) % (nyh * ny)
-        return (dp_of(z, there % ny, c), (there // ny) * nx + x)
-
     greet(sibling)
-    for way in range(2):
-        greet(along_y(way))
 
 
     quarter = acts.shape[0] // 4
@@ -136,16 +128,10 @@
             + rx[1 - half, NEAR, to_yh, piece]
         )
 
-    def m_copy(half, piece):
-        return remote(
-            cross.at[half, piece], mid.at[half, piece], m_send.at[half, piece],
-            m_recv.at[half, piece], along_y(half),
-        )
-
     def y_copy(half, piece):
         return remote(
-            mid.at[half, piece], ry.at[half, piece], y_send.at[half, piece],
-            y_recv.at[half, piece], along_y(half),
+            cross.at[half, piece], ry.at[half, piece], y_send.at[half, piece],
+            y_recv.at[half, piece], at_fsdp(other_yh * nx + x),
         )
 
     wide = ny * nc * ROWS
@@ -163,7 +149,7 @@
     project(opposite, other_yh)
     project(neighbour(0), other_yh)
     project(neighbour(1), other_yh)
-    pl.semaphore_wait(barrier, groups - 1 + ny - 1 + nz - 1 + 1 + 2)
+    pl.semaphore_wait(barrier, groups - 1 + ny - 1 + nz - 1 + 1)
     send_first(other_yh)
     project(x, other_yh)
     send_last(other_yh)
@@ -175,14 +161,10 @@
     for piece in range(2):
         for half in range(2):
             cross[half, piece] = x_total(other_yh, half, piece)
-            m_copy(half, piece).start()
+            y_copy(half, piece).start()
     send_last(yh)
     loads[2].wait()
     turn(0, nz // 2)
-    for piece in range(2):
-        for half in range(2):
-            m_copy(half, piece).wait_recv()
-            y_copy(half, piece).start()
     turn(nz // 2, nz)
     for piece in range(2):
         for half in range(2):
@@ -326,12 +308,13 @@
             d_recv.at[groups - k], at_fsdp((fs + k) % groups),
         ).wait_recv()
 
-    tile = basis.shape[0] // 4
-    first = pl.ds(0, 3 * tile)
-    second = pl.ds(3 * tile, tile)
+    tiles = basis.shape[0] // LANES
+    cut = tiles * 5 // 8
+    first = pl.ds(0, cut * LANES)
+    second = pl.ds(cut * LANES, (tiles - cut) * LANES)
 
     def update(j):
-        features = pl.ds(pl.multiple_of(j * tile, tile), tile)
+        features = pl.ds(pl.multiple_of(j * LANES, LANES), LANES)
         delta = jnp.dot(full_dir[...], basis_t[:, features], preferred_element_type=F32)
         updated = master[:, features] - 0.0125 * delta
         new_master[:, features] = updated
@@ -346,24 +329,35 @@
     def behind(way, step):
         return (z + nz - step) % nz if way == 0 else (z + step) % nz
 
-    def z4_copy(way, stage, ahead, k):
-        block = weight.at[behind(way, 2 * (stage - 1)), (y + k) % ny, c, :, first]
-        return remote(
-            block, block, z4_send, z4_recv.at[way, 2 * (stage - 1) + ahead, k],
-            at_dp(dp_of(behind(1 - way, ahead), y, c)),
-        )
+    def ring(hops):
+        starts = [sum(hops[:i]) for i in range(len(hops))]
+        return [(at, [at + ahead for ahead in range(hop, 0, -1)]) for at, hop in zip(starts, hops)]
+
+    ring_a = ring(FIRST_HOPS if half_z == 8 else (2,) * (half_z // 2))
+    ring_b = ring((2,) * (half_z // 2))
+
+    def z4_send_on(way, at, steps, k):
+        block = weight.at[behind(way, at), (y + k) % ny, c, :, first]
+        for step in steps:
+            if step < half_z or way == last_way(k):
+                remote(
+                    block, block, z4_send, z4_recv.at[way, step, k],
+                    at_dp(dp_of(behind(1 - way, step - at), y, c)),
+                ).start()
 
     def z4_wait(way, step, k):
         wait_bytes(
             weight.at[behind(way, step), (y + k) % ny, c, :, first], z4_recv.at[way, step, k]
         )
 
-    def b_copy(way, stage, ahead):
-        block = weight.at[behind(way, 2 * (stage - 1)), y, c, :, second]
-        return remote(
-            block, block, b_send, b_recv.at[way, 2 * (stage - 1) + ahead],
-            at_dp(dp_of(behind(1 - way, ahead), y, c)),
-        )
+    def b_send_on(way, at, steps):
+        block = weight.at[behind(way, at), y, c, :, second]
+        for step in steps:
+            if step < half_z or way == 0:
+                remote(
+                    block, block, b_send, b_recv.at[way, step],
+                    at_dp(dp_of(behind(1 - way, step - at), y, c)),
+                ).start()
 
     def b_wait(way, step):
         wait_bytes(weight.at[behind(way, step), y, c, :, second], b_recv.at[way, step])
@@ -400,78 +394,60 @@
     def last_way(k):
         return 0 if k < ny // 2 else 1
 
-    stages = half_z // 2
-
-    def onward(way, stage, copy, chosen):
-        if chosen:
-            copy(way, stage, 2).start()
-        else:
-            pl.when(stage < stages)(lambda: copy(way, stage, 2).start())
-        copy(way, stage, 1).start()
-
-    def z4_onward(way, stage, k):
-        onward(way, stage, lambda *args: z4_copy(*args, k), last_way(k) == way)
-
-    update(3)
+    def each_way(step):
+        return range(2) if step < half_z else range(1)
+
+    pl.loop(cut, tiles)(update)
     for way in range(2):
-        onward(way, jnp.int32(1), b_copy, way == 0)
+        b_send_on(way, *ring_b[0])
     spread(z)
-    pl.loop(0, 3)(update)
+    pl.loop(0, cut)(update)
     for k in range(ny):
         if k:
             y4_copy(ny - k).wait_recv()
         for way in range(2):
-            z4_onward(way, jnp.int32(1), k)
+            z4_send_on(way, *ring_a[0], k)
         if not k:
             for j in range(1, ny):
                 y4_copy(j).start()
     share(z)
 
-    @pl.loop(1, stages)
-    def _(stage):
-        for way in range(2):
-            b_wait(way, 2 * stage)
-            onward(way, stage + 1, b_copy, way == 0)
-        for k in range(ny):
-            for way in range(2):
-                z4_wait(way, 2 * stage, k)
-                z4_onward(way, stage + 1, k)
-        for way in range(2):
-            b_wait(way, 2 * stage - 1)
+    queue_b = list(zip(ring_b, ring_b[1:] + [None]))
+    stored = []
+    for (_, steps), onward in zip(ring_a, ring_a[1:] + [None]):
+        while queue_b and queue_b[0][0][1][0] <= max(steps[0], 2):
+            (_, b_steps), b_onward = queue_b.pop(0)
+            for step in b_steps:
+                for way in each_way(step):
+                    b_wait(way, step)
+                    if b_onward and step == b_onward[0]:
+                        b_send_on(way, *b_onward)
+            for step in b_steps:
+                for way in each_way(step):
+                    spread(behind(way, step))
+        for step in steps:
             for k in range(ny):
-                z4_wait(way, 2 * stage - 1, k)
-            for back in range(2):
-                spread(behind(way, 2 * stage - back))
-                share(behind(way, 2 * stage - back))
-
-        @pl.when(stage > 1)
-        def _():
-            for way in range(2):
-                for back in range(2, 4):
-                    store(behind(way, 2 * stage - back))
-
-    for way in range(2):
-        b_wait(way, half_z - 1)
-        spread(behind(way, half_z - 1))
-    b_wait(0, half_z)
-    spread(behind(0, half_z))
-    share_line(y)
-    for way in range(2):
-        for k in range(ny):
-            z4_wait(way, half_z - 1, k)
-        share(behind(way, half_z - 1))
-    for k in range(ny):
-        z4_wait(last_way(k), half_z, k)
-    share(behind(0, half_z))
+                for way in range(2):
+                    if step < half_z or way == last_way(k):
+                        z4_wait(way, step, k)
+                        if onward and step == onward[0]:
+                            z4_send_on(way, *onward, k)
+        for step in steps:
+            for way in each_way(step):
+                share(behind(way, step))
+        if not onward:
+            share_line(y)
+        while len(stored) > 4:
+            store(stored.pop(0))
+        stored += [behind(way, step) for step in reversed(steps) for way in each_way(step)]
+
     store(z)
-    for way in range(2):
-        for step in range(max(half_z - 3, 1), half_z):
-            store(behind(way, step))
+    for zz in stored:
+        store(zz)
     for k in range(1, ny):
         yy = (y + k) % ny
         wait_bytes(weight.at[:, yy, c, :, second], by_recv.at[k])
         share_line(yy)
-    store(behind(0, half_z))
     for k in range(ny):
         store_line((y + k) % ny)
 
@@ -482,7 +458,6 @@
                     x_copy(way, kind, to_yh, piece).wait_send()
     for half in range(2):
         for piece in range(2):
-            m_copy(half, piece).wait_send()
             y_copy(half, piece).wait_send()
 
     @pl.loop(0, ny)
@@ -558,7 +533,6 @@
             pltpu.VMEM((2, 3, nyh, 2, quarter, LANES), F32),
             pltpu.VMEM((2, 2, quarter, LANES), F32),
             pltpu.VMEM((2, 2, quarter, LANES), F32),
-            pltpu.VMEM((2, 2, quarter, LANES), F32),
             pltpu.VMEM(grad_out.shape, BF16),
             pltpu.VMEM((nc, ny, nz, ROWS, tokens), BF16),
             pltpu.VMEM((tokens, LANES), BF16),
@@ -574,7 +548,6 @@
             pltpu.VMEM((ROWS, groups * LANES), BF16),
             dma((6,)),
             dma((2, 3, nyh, 2)), dma((2, 3, nyh, 2)),
-            dma((2, 2)), dma((2, 2)),
             dma((2, 2)), dma((2, 2)),
             dma((ny,)), dma((ny,)),
             dma((ny,)), dma((ny,)),

time: 112 us -> 107 us (0.955)
  Pallas kernels: 112 us -> 106 us
    pallas_call x1, Pallas kernels: 108 us -> 102 us  [on_device(): pl.pallas_call(functools.partial(kernel, sizes), out_shape=(shape((ROWS,...]
where the time goes in v3:
time: 107 us
  Pallas kernels  106 us (99%)
    pallas_call x1, Pallas kernels, on_device(): pl.pallas_call(functools.partial(kernel, sizes), out_shape=(shape((ROWS,...  102 us
    pallas_call x1, Pallas kernels, on_device(): pl.pallas_call(deliver, out_shape=[shape(r.shape, r.dtype) for r in resul...  4.05 us

profile of v3, /device:TPU:1, one launch (start us, length us, event | category | flops | bytes accessed | tf_op | source)
XLA Modules:
  0.0 106.7 jit_solution(14616499786688217419)
XLA Ops:
  0.6 102.0 %galore_step.1 = (f32[16,1024]{1,0:T(8,128)}, bf16[16,4,2,16,1024]{4,3,2,1,0:T(8,128)(2,1)}, f32[16,128]{1,0:T(8,128)}, f32[16,128]{1,0:T(8,128)}) custom-call(bf16[384,1024]{1,0:T(8,128)(2,1)} %acts_h.1, bf16[384,2048]{1,0:T(8,128)(2,1)} %grad.1, bf16[1024,1024]{1,0:T(8,128)(2,1)} %basis_h.1, f32[16,1024]{1,0:T(8,128)} %master_h.1, f32[16,128]{1,0:T(8,128)} %avg_h.1, ...), custom_call_target="tpu_custom_call" | custom-call | flops 1006632960 | bytes 16777216 | tf_op jit(solution)/shard_map/galore_step/pallas_call | solution.py:515
  102.7 4.1 %deliver.1 = (f32[16,1024]{1,0:T(8,128)}, bf16[16,4,2,16,1024]{4,3,2,1,0:T(8,128)(2,1)}, f32[16,128]{1,0:T(8,128)}, f32[16,128]{1,0:T(8,128)}) custom-call(f32[16,1024]{1,0:T(8,128)} %get-tuple-element.12.master, bf16[16,4,2,16,1024]{4,3,2,1,0:T(8,128)(2,1)} %get-tuple-element.13.weight, f32[16,128]{1,0:T(8,128)} %get-tuple-element.14.avg, ...), custom_call_target="tpu_custom_call" | custom-call | tf_op jit(solution)/shard_map/deliver/pallas_call | solution.py:573
